TPU v7x, 256 devices: a whole 4x4x8 slice. The times are simulated.
256 devices in a mesh: section: 16 (over z_lo, y), dp: 16 (over x, z_hi, core).
Axes of the slice: x: 4, y: 4, z: 8 (z_hi: 2, z_lo: 4; z = z_hi * 4 + z_lo), core: 2. Of those that a mesh axis runs over, the one named last changes fastest.
Arguments:
- layer_inputs: bfloat16 [16, 2, 64, 4096], P('section'), may hold values from -6 to 6
- top_grad: bfloat16 [2, 64, 4096], replicated, may hold values from -3 to 3
- w_query: bfloat16 [16, 4096, 4096], P('section', None, 'dp'), may hold values from -1 to 1
- w_keyval: bfloat16 [16, 4096, 1024], P('section', None, 'dp'), may hold values from -1 to 1
- w_out: bfloat16 [16, 4096, 4096], P('section', 'dp'), may hold values from -0.02734375 to 0.02734375
- norm_gain: bfloat16 [16, 4096], P('section'), may hold values from 0.25 to 1.75
- new_block: int32 [16], P('section'), may hold values 0 or 1
Outputs:
- grad_stream: bfloat16 [16, 2, 64, 4096], P('section', None, None, 'dp')
- grad_out_proj: float32 [16, 4096, 4096], P('section', 'dp')
All inputs are finite; a program needn't handle non-finite values. No bound on the sum of `new_block` on one device may be relied on, other than what follows from the above.
Results may differ from a plain program's by a relative error of at most 0.035.
Values may be sent and summed in bfloat16 or wider, within the bound.
A program may use at most 64 MiB of HBM per device.

v0:
```python
import jax
import jax.numpy as jnp
from jax import lax
from jax.sharding import PartitionSpec as P

KVH = 4
HEAD_DIM = 128


EPS = 1e-05


def swapped(value, axis, distance):
    mask = 2**distance
    pairs = [(source, source ^ mask) for source in range(lax.axis_size(axis))]
    return lax.ppermute(value, axis, pairs)


def shifted(value, axis, by):
    count = lax.axis_size(axis)
    pairs = [(i, i + by) for i in range(count) if 0 <= i + by < count]
    return lax.ppermute(value, axis, pairs)


def body(layer_inputs, top_grad, w_query, w_keyval, w_out, norm_gain, new_block):
    dp_count = lax.axis_size("dp")
    section_count = lax.axis_size("section")
    dp_pos = lax.axis_index("dp")
    section_pos = lax.axis_index("section")
    micro_count = layer_inputs.shape[1]
    tokens = layer_inputs.shape[2]
    width = layer_inputs.shape[3]
    slice_width = width // dp_count
    query_local = w_query[0]
    out_local = w_out[0]
    gain = norm_gain[0].astype(jnp.float32)
    is_new = new_block[0] == 1
    scale_factor = HEAD_DIM ** (-0.5)
    local_heads = query_local.shape[1] // HEAD_DIM
    head_cols = w_keyval[0]
    for bit_pos in range((dp_count // KVH).bit_length() - 1):
        partner = swapped(head_cols, "dp", bit_pos)
        lower = dp_pos // 2**bit_pos % 2 == 0
        head_cols = jnp.where(
            lower,
            jnp.concatenate([head_cols, partner], 1),
            jnp.concatenate([partner, head_cols], 1),
        )
    causal = jnp.arange(tokens)[:, None] >= jnp.arange(tokens)[None, :]
    col_start = dp_pos * slice_width
    top_section = section_pos == section_count - 1

    def layer_terms(inputs, upstream):
        inputs_f = inputs.astype(jnp.float32)
        inverse_rms = lax.rsqrt(jnp.mean(inputs_f * inputs_f, axis=-1, keepdims=True) + EPS)
        normed = (inputs_f * inverse_rms * gain).astype(jnp.bfloat16)
        queries = jnp.dot(normed, query_local, preferred_element_type=jnp.float32).astype(
            jnp.bfloat16
        )
        queries = queries.reshape(tokens, local_heads, HEAD_DIM)
        keyval = jnp.dot(normed, head_cols, preferred_element_type=jnp.float32).astype(jnp.bfloat16)
        key_rows = keyval[:, :HEAD_DIM]
        value_rows = keyval[:, HEAD_DIM:]
        scores = (
            jnp.einsum("thd,sd->hts", queries, key_rows, preferred_element_type=jnp.float32)
            * scale_factor
        )
        scores = jnp.where(causal[None], scores, -1e30)
        probs = jax.nn.softmax(scores, axis=-1)
        probs_low = probs.astype(jnp.bfloat16)
        attended = jnp.einsum(
            "hts,sd->thd", probs_low, value_rows, preferred_element_type=jnp.float32
        ).astype(jnp.bfloat16)
        attended_flat = attended.reshape(tokens, local_heads * HEAD_DIM)
        out_grad = jnp.einsum(
            "tc,kc->tk", upstream, out_local, preferred_element_type=jnp.float32
        ).astype(jnp.bfloat16)
        out_grad = out_grad.reshape(tokens, local_heads, HEAD_DIM)
        weight_grad = jnp.einsum(
            "tk,tc->kc", attended_flat, upstream, preferred_element_type=jnp.float32
        )
        prob_grad = jnp.einsum(
            "thd,sd->hts", out_grad, value_rows, preferred_element_type=jnp.float32
        )
        row_delta = jnp.sum(probs * prob_grad, axis=-1, keepdims=True)
        score_low = (probs * (prob_grad - row_delta)).astype(jnp.bfloat16)
        query_grad = (
            jnp.einsum("hts,sd->thd", score_low, key_rows, preferred_element_type=jnp.float32)
            * scale_factor
        )
        query_grad = query_grad.astype(jnp.bfloat16).reshape(tokens, local_heads * HEAD_DIM)
        key_grad = (
            jnp.einsum("hts,thd->sd", score_low, queries, preferred_element_type=jnp.float32)
            * scale_factor
        )
        value_grad = jnp.einsum(
            "hts,thd->sd", probs_low, out_grad, preferred_element_type=jnp.float32
        )
        keyval_grad = jnp.concatenate([key_grad, value_grad], axis=-1).astype(jnp.bfloat16)
        partial_value = jnp.einsum(
            "tk,ck->tc", query_grad, query_local, preferred_element_type=jnp.float32
        )
        partial_value = partial_value + jnp.einsum(
            "tk,ck->tc", keyval_grad, head_cols, preferred_element_type=jnp.float32
        )
        return (partial_value, weight_grad, inputs_f, inverse_rms)

    def backward_step(step_pos, received):
        micro_pos = step_pos - (section_count - 1 - section_pos)
        active = (micro_pos >= 0) & (micro_pos < micro_count)
        micro_clip = jnp.clip(micro_pos, 0, micro_count - 1)
        inputs = lax.dynamic_index_in_dim(layer_inputs[0], micro_clip, 0, keepdims=False)
        from_top = lax.dynamic_index_in_dim(top_grad, micro_clip, 0, keepdims=False)
        upstream = jnp.where(top_section, from_top, received)
        partial_value, weight_grad, inputs_f, inverse_rms = layer_terms(inputs, upstream)
        summed = lax.psum_scatter(
            partial_value.astype(jnp.bfloat16), "dp", scatter_dimension=1, tiled=True
        )
        return (summed, upstream, weight_grad, inputs_f, inverse_rms, micro_clip, active)

    def record(stream_acc, grad_acc, result_part, weight_grad, micro_clip, active):
        old_row = lax.dynamic_index_in_dim(stream_acc, micro_clip, 0, keepdims=False)
        new_row = jnp.where(active, result_part, old_row)
        stream_acc = lax.dynamic_update_index_in_dim(stream_acc, new_row, micro_clip, 0)
        grad_acc = grad_acc + jnp.where(active & is_new, weight_grad, 0.0)
        return (stream_acc, grad_acc)

    stream_init = jnp.zeros((micro_count, tokens, slice_width), jnp.bfloat16)
    grad_init = jnp.zeros((out_local.shape[0], width), jnp.float32)
    tick_count = micro_count + section_count - 1

    def tick_whole(step_pos, carry):
        incoming, stream_acc, grad_acc = carry
        norm_part, upstream, weight_grad, inputs_f, inverse_rms, micro_clip, active = backward_step(
            step_pos, incoming
        )
        norm_grad = lax.all_gather(norm_part, "dp", axis=1, tiled=True).astype(jnp.float32)
        scaled = norm_grad * gain
        row_stat = jnp.sum(scaled * inputs_f, axis=-1, keepdims=True) / width
        result = (
            upstream.astype(jnp.float32)
            + inverse_rms * scaled
            - inputs_f * inverse_rms**3 * row_stat
        ).astype(jnp.bfloat16)
        outgoing = shifted(result, "section", -1)
        result_part = lax.dynamic_slice_in_dim(result, col_start, slice_width, 1)
        stream_acc, grad_acc = record(
            stream_acc, grad_acc, result_part, weight_grad, micro_clip, active
        )
        return (outgoing, stream_acc, grad_acc)

    start = jnp.zeros((tokens, width), jnp.bfloat16)
    carry = lax.fori_loop(0, tick_count, tick_whole, (start, stream_init, grad_init))
    return (carry[1][None], carry[2][None])


def solution(mesh):
    in_specs = (
        P("section", None, None, None),
        P(),
        P("section", None, "dp"),
        P("section", None, "dp"),
        P("section", "dp", None),
        P("section", None),
        P("section"),
    )
    out_specs = (P("section", None, None, "dp"), P("section", "dp", None))
    return jax.shard_map(body, mesh=mesh, in_specs=in_specs, out_specs=out_specs, check_vma=False)
```

profile of v0, /device:TPU:1, one launch (start us, length us, event | category | flops | bytes accessed | tf_op | source)
XLA Modules:
  0.0 2369.8 jit_solution(1513456460127013355)
XLA Ops:
  53.4 2309.2 %while.20 = (s32[]{:T(128)}, bf16[64,4096]{1,0:T(8,128)(2,1)S(1)}, bf16[2,64,256]{2,1,0:T(8,128)(2,1)S(1)}, f32[256,4096]{1,0:T(8,128)}, pred[]{:T(512)}, /*inde...) while((s32[]{:T(128)}, bf16[64,4096]{1,0:T(8,128)(2,1)S(1)}, ...), condition=%wide.region_7.8_spmd.clone, body=%wide.region_0.7_spmd.clone.sunk | while | flops 828969088 | bytes 55234480 | solution.py:153
  64.4 92.5 %reduce-scatter.2.cloned.1.call-done = bf16[64,256]{1,0:T(8,128)(2,1)} async-done(((bf16[64,4096]{1,0:T(8,128)(2,1)}), bf16[64,256]{1,0:T(8,128)(2,1)}) %reduce-scatter.2.cloned.1.call-update) | async-done | bytes 32784 | tf_op jit(solution)/shard_map/while/body/eval_jaxpr/reduce_scatter | solution.py:116
  217.1 74.7 %reduce-scatter.2.cloned.1.call-done = bf16[64,256]{1,0:T(8,128)(2,1)} async-done(((bf16[64,4096]{1,0:T(8,128)(2,1)}), bf16[64,256]{1,0:T(8,128)(2,1)}) %reduce-scatter.2.cloned.1.call-update) | async-done | bytes 32784 | tf_op jit(solution)/shard_map/while/body/eval_jaxpr/reduce_scatter | solution.py:116
  291.7 31.3 %all_gather.11 = bf16[64,4096]{1,0:T(8,128)(2,1)S(1)} all-gather(bf16[64,256]{1,0:T(8,128)(2,1)} %reduce-scatter.2.cloned.1.call-done), channel_id=1, replica_groups=mesh['section'=16,'dp'=16] {'dp'}, dimensions={1}, use_global_device_ids=true | all-gather | bytes 557056 | tf_op jit(solution)/shard_map/while/body/eval_jaxpr/all_gather | solution.py:137
  351.9 74.6 %reduce-scatter.2.cloned.1.call-done = bf16[64,256]{1,0:T(8,128)(2,1)} async-done(((bf16[64,4096]{1,0:T(8,128)(2,1)}), bf16[64,256]{1,0:T(8,128)(2,1)}) %reduce-scatter.2.cloned.1.call-update) | async-done | bytes 32784 | tf_op jit(solution)/shard_map/while/body/eval_jaxpr/reduce_scatter | solution.py:116
  486.8 74.3 %reduce-scatter.2.cloned.1.call-done = bf16[64,256]{1,0:T(8,128)(2,1)} async-done(((bf16[64,4096]{1,0:T(8,128)(2,1)}), bf16[64,256]{1,0:T(8,128)(2,1)}) %reduce-scatter.2.cloned.1.call-update) | async-done | bytes 32784 | tf_op jit(solution)/shard_map/while/body/eval_jaxpr/reduce_scatter | solution.py:116
  561.1 31.3 %all_gather.11 = bf16[64,4096]{1,0:T(8,128)(2,1)S(1)} all-gather(bf16[64,256]{1,0:T(8,128)(2,1)} %reduce-scatter.2.cloned.1.call-done), channel_id=1, replica_groups=mesh['section'=16,'dp'=16] {'dp'}, dimensions={1}, use_global_device_ids=true | all-gather | bytes 557056 | tf_op jit(solution)/shard_map/while/body/eval_jaxpr/all_gather | solution.py:137
  621.3 74.6 %reduce-scatter.2.cloned.1.call-done = bf16[64,256]{1,0:T(8,128)(2,1)} async-done(((bf16[64,4096]{1,0:T(8,128)(2,1)}), bf16[64,256]{1,0:T(8,128)(2,1)}) %reduce-scatter.2.cloned.1.call-update) | async-done | bytes 32784 | tf_op jit(solution)/shard_map/while/body/eval_jaxpr/reduce_scatter | solution.py:116
  756.1 74.3 %reduce-scatter.2.cloned.1.call-done = bf16[64,256]{1,0:T(8,128)(2,1)} async-done(((bf16[64,4096]{1,0:T(8,128)(2,1)}), bf16[64,256]{1,0:T(8,128)(2,1)}) %reduce-scatter.2.cloned.1.call-update) | async-done | bytes 32784 | tf_op jit(solution)/shard_map/while/body/eval_jaxpr/reduce_scatter | solution.py:116
  830.4 31.3 %all_gather.11 = bf16[64,4096]{1,0:T(8,128)(2,1)S(1)} all-gather(bf16[64,256]{1,0:T(8,128)(2,1)} %reduce-scatter.2.cloned.1.call-done), channel_id=1, replica_groups=mesh['section'=16,'dp'=16] {'dp'}, dimensions={1}, use_global_device_ids=true | all-gather | bytes 557056 | tf_op jit(solution)/shard_map/while/body/eval_jaxpr/all_gather | solution.py:137
  890.7 74.3 %reduce-scatter.2.cloned.1.call-done = bf16[64,256]{1,0:T(8,128)(2,1)} async-done(((bf16[64,4096]{1,0:T(8,128)(2,1)}), bf16[64,256]{1,0:T(8,128)(2,1)}) %reduce-scatter.2.cloned.1.call-update) | async-done | bytes 32784 | tf_op jit(solution)/shard_map/while/body/eval_jaxpr/reduce_scatter | solution.py:116
  965.0 31.3 %all_gather.11 = bf16[64,4096]{1,0:T(8,128)(2,1)S(1)} all-gather(bf16[64,256]{1,0:T(8,128)(2,1)} %reduce-scatter.2.cloned.1.call-done), channel_id=1, replica_groups=mesh['section'=16,'dp'=16] {'dp'}, dimensions={1}, use_global_device_ids=true | all-gather | bytes 557056 | tf_op jit(solution)/shard_map/while/body/eval_jaxpr/all_gather | solution.py:137
  1025.2 74.6 %reduce-scatter.2.cloned.1.call-done = bf16[64,256]{1,0:T(8,128)(2,1)} async-done(((bf16[64,4096]{1,0:T(8,128)(2,1)}), bf16[64,256]{1,0:T(8,128)(2,1)}) %reduce-scatter.2.cloned.1.call-update) | async-done | bytes 32784 | tf_op jit(solution)/shard_map/while/body/eval_jaxpr/reduce_scatter | solution.py:116
  1160.1 74.6 %reduce-scatter.2.cloned.1.call-done = bf16[64,256]{1,0:T(8,128)(2,1)} async-done(((bf16[64,4096]{1,0:T(8,128)(2,1)}), bf16[64,256]{1,0:T(8,128)(2,1)}) %reduce-scatter.2.cloned.1.call-update) | async-done | bytes 32784 | tf_op jit(solution)/shard_map/while/body/eval_jaxpr/reduce_scatter | solution.py:116
  1294.9 74.7 %reduce-scatter.2.cloned.1.call-done = bf16[64,256]{1,0:T(8,128)(2,1)} async-done(((bf16[64,4096]{1,0:T(8,128)(2,1)}), bf16[64,256]{1,0:T(8,128)(2,1)}) %reduce-scatter.2.cloned.1.call-update) | async-done | bytes 32784 | tf_op jit(solution)/shard_map/while/body/eval_jaxpr/reduce_scatter | solution.py:116
  1429.8 74.6 %reduce-scatter.2.cloned.1.call-done = bf16[64,256]{1,0:T(8,128)(2,1)} async-done(((bf16[64,4096]{1,0:T(8,128)(2,1)}), bf16[64,256]{1,0:T(8,128)(2,1)}) %reduce-scatter.2.cloned.1.call-update) | async-done | bytes 32784 | tf_op jit(solution)/shard_map/while/body/eval_jaxpr/reduce_scatter | solution.py:116
  1564.6 74.4 %reduce-scatter.2.cloned.1.call-done = bf16[64,256]{1,0:T(8,128)(2,1)} async-done(((bf16[64,4096]{1,0:T(8,128)(2,1)}), bf16[64,256]{1,0:T(8,128)(2,1)}) %reduce-scatter.2.cloned.1.call-update) | async-done | bytes 32784 | tf_op jit(solution)/shard_map/while/body/eval_jaxpr/reduce_scatter | solution.py:116
  1639.0 31.3 %all_gather.11 = bf16[64,4096]{1,0:T(8,128)(2,1)S(1)} all-gather(bf16[64,256]{1,0:T(8,128)(2,1)} %reduce-scatter.2.cloned.1.call-done), channel_id=1, replica_groups=mesh['section'=16,'dp'=16] {'dp'}, dimensions={1}, use_global_device_ids=true | all-gather | bytes 557056 | tf_op jit(solution)/shard_map/while/body/eval_jaxpr/all_gather | solution.py:137
  1699.2 74.7 %reduce-scatter.2.cloned.1.call-done = bf16[64,256]{1,0:T(8,128)(2,1)} async-done(((bf16[64,4096]{1,0:T(8,128)(2,1)}), bf16[64,256]{1,0:T(8,128)(2,1)}) %reduce-scatter.2.cloned.1.call-update) | async-done | bytes 32784 | tf_op jit(solution)/shard_map/while/body/eval_jaxpr/reduce_scatter | solution.py:116
  1773.9 31.3 %all_gather.11 = bf16[64,4096]{1,0:T(8,128)(2,1)S(1)} all-gather(bf16[64,256]{1,0:T(8,128)(2,1)} %reduce-scatter.2.cloned.1.call-done), channel_id=1, replica_groups=mesh['section'=16,'dp'=16] {'dp'}, dimensions={1}, use_global_device_ids=true | all-gather | bytes 557056 | tf_op jit(solution)/shard_map/while/body/eval_jaxpr/all_gather | solution.py:137
  1834.2 74.6 %reduce-scatter.2.cloned.1.call-done = bf16[64,256]{1,0:T(8,128)(2,1)} async-done(((bf16[64,4096]{1,0:T(8,128)(2,1)}), bf16[64,256]{1,0:T(8,128)(2,1)}) %reduce-scatter.2.cloned.1.call-update) | async-done | bytes 32784 | tf_op jit(solution)/shard_map/while/body/eval_jaxpr/reduce_scatter | solution.py:116
  1969.0 74.6 %reduce-scatter.2.cloned.1.call-done = bf16[64,256]{1,0:T(8,128)(2,1)} async-done(((bf16[64,4096]{1,0:T(8,128)(2,1)}), bf16[64,256]{1,0:T(8,128)(2,1)}) %reduce-scatter.2.cloned.1.call-update) | async-done | bytes 32784 | tf_op jit(solution)/shard_map/while/body/eval_jaxpr/reduce_scatter | solution.py:116
  2103.9 74.6 %reduce-scatter.2.cloned.1.call-done = bf16[64,256]{1,0:T(8,128)(2,1)} async-done(((bf16[64,4096]{1,0:T(8,128)(2,1)}), bf16[64,256]{1,0:T(8,128)(2,1)}) %reduce-scatter.2.cloned.1.call-update) | async-done | bytes 32784 | tf_op jit(solution)/shard_map/while/body/eval_jaxpr/reduce_scatter | solution.py:116
  2238.7 74.6 %reduce-scatter.2.cloned.1.call-done = bf16[64,256]{1,0:T(8,128)(2,1)} async-done(((bf16[64,4096]{1,0:T(8,128)(2,1)}), bf16[64,256]{1,0:T(8,128)(2,1)}) %reduce-scatter.2.cloned.1.call-update) | async-done | bytes 32784 | tf_op jit(solution)/shard_map/while/body/eval_jaxpr/reduce_scatter | solution.py:116
  (570 shorter events, 879.2 us)
Async XLA Ops:
  13.7 34.5 %collective-permute-start.2 = (bf16[4096,128]{0,1:T(8,128)(2,1)S(1)}, bf16[4096,128]{0,1:T(8,128)(2,1)S(1)}, u32[]{:S(2)}, u32[]{:S(2)}) collective-permute-start(bf16[4096,128]{0,1:T(8,128)(2,1)S(1)} %maximum_select_fusion.1), channel_id=1, source_target_pairs={{0,2},{1,3},{2,0},{3,1},{4,6},{5,7},{6,4},{7,5},{8,10},{9,11},{10,... | collective-permute-start | bytes 3145736 | tf_op jit(solution)/shard_map/ppermute | solution.py:16
  53.4 103.4 %reduce-scatter.2.cloned.1.call-start = ((), (), s32[]{:S(2)}) async-start(), calls=%async_computation.1 | async-start | bytes 557056 | tf_op jit(solution)/shard_map/while/body/eval_jaxpr/reduce_scatter | solution.py:116
  206.1 85.6 %reduce-scatter.2.cloned.1.call-start = ((), (), s32[]{:S(2)}) async-start(), calls=%async_computation.1 | async-start | bytes 557056 | tf_op jit(solution)/shard_map/while/body/eval_jaxpr/reduce_scatter | solution.py:116
  341.0 85.5 %reduce-scatter.2.cloned.1.call-start = ((), (), s32[]{:S(2)}) async-start(), calls=%async_computation.1 | async-start | bytes 557056 | tf_op jit(solution)/shard_map/while/body/eval_jaxpr/reduce_scatter | solution.py:116
  475.8 85.2 %reduce-scatter.2.cloned.1.call-start = ((), (), s32[]{:S(2)}) async-start(), calls=%async_computation.1 | async-start | bytes 557056 | tf_op jit(solution)/shard_map/while/body/eval_jaxpr/reduce_scatter | solution.py:116
  610.4 85.6 %reduce-scatter.2.cloned.1.call-start = ((), (), s32[]{:S(2)}) async-start(), calls=%async_computation.1 | async-start | bytes 557056 | tf_op jit(solution)/shard_map/while/body/eval_jaxpr/reduce_scatter | solution.py:116
  729.9 15.3 collective-permute-start
  745.2 85.2 %reduce-scatter.2.cloned.1.call-start = ((), (), s32[]{:S(2)}) async-start(), calls=%async_computation.1 | async-start | bytes 557056 | tf_op jit(solution)/shard_map/while/body/eval_jaxpr/reduce_scatter | solution.py:116
  879.7 85.3 %reduce-scatter.2.cloned.1.call-start = ((), (), s32[]{:S(2)}) async-start(), calls=%async_computation.1 | async-start | bytes 557056 | tf_op jit(solution)/shard_map/while/body/eval_jaxpr/reduce_scatter | solution.py:116
  999.0 15.3 collective-permute-start
  1014.3 85.6 %reduce-scatter.2.cloned.1.call-start = ((), (), s32[]{:S(2)}) async-start(), calls=%async_computation.1 | async-start | bytes 557056 | tf_op jit(solution)/shard_map/while/body/eval_jaxpr/reduce_scatter | solution.py:116
  1133.9 15.3 collective-permute-start
  1149.1 85.6 %reduce-scatter.2.cloned.1.call-start = ((), (), s32[]{:S(2)}) async-start(), calls=%async_computation.1 | async-start | bytes 557056 | tf_op jit(solution)/shard_map/while/body/eval_jaxpr/reduce_scatter | solution.py:116
  1268.7 15.3 collective-permute-start
  1284.0 85.7 %reduce-scatter.2.cloned.1.call-start = ((), (), s32[]{:S(2)}) async-start(), calls=%async_computation.1 | async-start | bytes 557056 | tf_op jit(solution)/shard_map/while/body/eval_jaxpr/reduce_scatter | solution.py:116
  1403.6 15.3 collective-permute-start
  1418.9 85.5 %reduce-scatter.2.cloned.1.call-start = ((), (), s32[]{:S(2)}) async-start(), calls=%async_computation.1 | async-start | bytes 557056 | tf_op jit(solution)/shard_map/while/body/eval_jaxpr/reduce_scatter | solution.py:116
  1538.4 15.3 collective-permute-start
  1553.7 85.3 %reduce-scatter.2.cloned.1.call-start = ((), (), s32[]{:S(2)}) async-start(), calls=%async_computation.1 | async-start | bytes 557056 | tf_op jit(solution)/shard_map/while/body/eval_jaxpr/reduce_scatter | solution.py:116
  1688.3 85.7 %reduce-scatter.2.cloned.1.call-start = ((), (), s32[]{:S(2)}) async-start(), calls=%async_computation.1 | async-start | bytes 557056 | tf_op jit(solution)/shard_map/while/body/eval_jaxpr/reduce_scatter | solution.py:116
  1823.2 85.6 %reduce-scatter.2.cloned.1.call-start = ((), (), s32[]{:S(2)}) async-start(), calls=%async_computation.1 | async-start | bytes 557056 | tf_op jit(solution)/shard_map/while/body/eval_jaxpr/reduce_scatter | solution.py:116
  1958.1 85.6 %reduce-scatter.2.cloned.1.call-start = ((), (), s32[]{:S(2)}) async-start(), calls=%async_computation.1 | async-start | bytes 557056 | tf_op jit(solution)/shard_map/while/body/eval_jaxpr/reduce_scatter | solution.py:116
  2092.9 85.6 %reduce-scatter.2.cloned.1.call-start = ((), (), s32[]{:S(2)}) async-start(), calls=%async_computation.1 | async-start | bytes 557056 | tf_op jit(solution)/shard_map/while/body/eval_jaxpr/reduce_scatter | solution.py:116
  2227.8 85.6 %reduce-scatter.2.cloned.1.call-start = ((), (), s32[]{:S(2)}) async-start(), calls=%async_computation.1 | async-start | bytes 557056 | tf_op jit(solution)/shard_map/while/body/eval_jaxpr/reduce_scatter | solution.py:116
  (65 other events, 327.9 us)
Sparse Core Ops, SparseCore 0:
  64.3 92.5 reduce-scatter.1
  216.9 74.7 reduce-scatter.1
  351.8 74.6 reduce-scatter.1
  486.7 74.3 reduce-scatter.1
  621.2 74.7 reduce-scatter.1
  756.0 74.3 reduce-scatter.1
  890.5 74.4 reduce-scatter.1
  1025.1 74.7 reduce-scatter.1
  1160.0 74.7 reduce-scatter.1
  1294.8 74.7 reduce-scatter.1
  1429.7 74.6 reduce-scatter.1
  1564.5 74.4 reduce-scatter.1
  1699.1 74.7 reduce-scatter.1
  1834.1 74.7 reduce-scatter.1
  1968.9 74.7 reduce-scatter.1
  2103.7 74.7 reduce-scatter.1
  2238.6 74.7 reduce-scatter.1
where the time goes:
time: 2380 us; the launch traced here: 2370 us
  waiting for transfers between devices  1470 us (62%)
  blocking collectives  531 us (22%)
  matrix products  239 us (10%)
  other arithmetic  75.6 us (3%)
  starting transfers between devices  30.6 us (1%)
    reduce_scatter x17, waiting for transfers between devices, backward_step(): lax.psum_scatter(partial_value.astype(jnp.bfloat16), 'dp', scatter_dimens...  1290 us
    all_gather x17, blocking collectives, tick_whole(): lax.all_gather(norm_part, 'dp', axis=1, tiled=True).astype(jnp.float32)  531 us
    ppermute x17, waiting for transfers between devices, shifted(): return lax.ppermute(value, axis, pairs)  155 us
    dot_general x17, matrix products, layer_terms(): jnp.einsum('tk,tc->kc', attended_flat, upstream, preferred_element_type=j...  81.8 us
  transfers between devices with their start and end apart: 36, of which 36 were waited for; matrix products, arithmetic and copies ran while one was open for 4% of the time, Pallas kernels for 0%

commit v1 on v0

v1 whole, which is shorter than its diff:
```python
import jax
import jax.numpy as jnp
from jax import lax
from jax.experimental import pallas as pl
from jax.experimental.pallas import tpu as pltpu
from jax.sharding import PartitionSpec as P

HEAD_DIM = 128
EPS = 1e-05
MESH = pl.DeviceIdType.MESH
F32 = jnp.float32
BF16 = jnp.bfloat16

SECTIONS = 16
TOKENS = 64
MICRO = 2
WIDTH = 4096
ROWS = 16
PARTS = TOKENS // ROWS
CHUNKS = MICRO * PARTS
LAG = 2
BLOCK = 256
SLICE = 2 * BLOCK
SCALE = HEAD_DIM ** (-0.5)

SLICES = [(2, 1), (2, 0), (1, 1), (1, 0), (3, 1), (3, 0), (0, 1), (0, 0)]
PEERS = [(dx, dz, dc) for dx, dc in SLICES for dz in (1, 0)][:-1]


def dot(a, b, ca=1, cb=0):
    return lax.dot_general(a, b, (((ca,), (cb,)), ((), ())), preferred_element_type=F32)


def columns(block):
    return pl.ds(pl.multiple_of(block * BLOCK, BLOCK), BLOCK)


def slice_blocks(index):
    return [(index // 2) * 4 + half * 2 + index % 2 for half in range(2)]


def kernel(
    x_ref, top_ref, wq_ref, wkv_ref, wo_ref, gain_ref,
    out_ref, grad_ref,
    wc, wot, normed, r_buf, q_hat, q_low, kv_hat, k_low, v_low, p_buf, p_low, att, dkv_acc,
    g_buf, part_buf, rs_buf, ag_buf, grad_buf,
    rs_send, rs_recv, ag_send, ag_recv, kv_send, kv_recv, grad_sem, gate,
):
    s = lax.axis_index("section")
    d = lax.axis_index("dp")
    x_pos = d // 4
    z_pos = d // 2 % 2
    c_pos = d % 2

    def peer(dx, dz, dc):
        return (x_pos + dx) % 4 * 4 + (z_pos + dz) % 2 * 2 + (c_pos + dc) % 2

    barrier = pltpu.get_barrier_semaphore()

    def greet(section, device):
        pl.semaphore_signal(barrier, inc=1, device_id=(section, device), device_id_type=MESH)

    for offset in PEERS:
        greet(s, peer(*offset))

    @pl.when(s > 0)
    def _():
        for dx, dc in SLICES:
            greet(s - 1, peer(dx, 0, dc))

    @pl.when(s < SECTIONS - 1)
    def _():
        for dx, dc in SLICES:
            greet(s + 1, peer(dx, 0, dc))

    @pl.when(s < SECTIONS - 4)
    def _():
        greet(s + 4, d)

    kv_row = pl.multiple_of(BLOCK + (z_pos * 2 + c_pos) * 64, 64)
    for b in range(WIDTH // BLOCK):
        rows = slice(b * BLOCK, (b + 1) * BLOCK)
        wc[pl.ds(kv_row, 64), rows] = wkv_ref[rows, :].T

    greetings = (
        len(PEERS)
        + jnp.where(s > 0, len(SLICES), 0)
        + jnp.where(s < SECTIONS - 1, len(SLICES), 0)
        + jnp.where(s >= 4, 1, 0)
    )
    pl.semaphore_wait(barrier, greetings)

    def kv_copy(row, device, sem):
        part = wc.at[pl.ds(row, 64)]
        return pltpu.make_async_remote_copy(
            src_ref=part, dst_ref=part, send_sem=kv_send.at[sem], recv_sem=kv_recv.at[sem],
            device_id=(s, device), device_id_type=MESH,
        )

    own_near = kv_copy(kv_row, peer(0, 0, 1), 0)
    own_near.start()

    @pl.when(s < SECTIONS - 4)
    def _():
        pl.semaphore_wait(gate, 1)

    own_far = kv_copy(kv_row, peer(0, 1, 0), 1)
    own_far.start()

    for i in range(CHUNKS):
        m, first = i % 2, (PARTS - 1 - i // 2) * ROWS
        xf = x_ref[m, first : first + ROWS, :].astype(F32)
        r = lax.rsqrt(jnp.mean(xf * xf, axis=-1, keepdims=True) + EPS)
        r_buf[i] = r
        normed[i * ROWS : (i + 1) * ROWS, :] = (xf * r * gain_ref[...]).astype(BF16)
    queries = dot(normed[...], wq_ref[...])
    for i in range(CHUNKS):
        rows = slice(i * ROWS, (i + 1) * ROWS)
        for h in range(2):
            part = queries[rows, h * HEAD_DIM : (h + 1) * HEAD_DIM]
            q_hat[i, h * ROWS : (h + 1) * ROWS, :] = part
            q_low[i, h * ROWS : (h + 1) * ROWS, :] = part.astype(BF16)
    for b in range(WIDTH // BLOCK):
        rows = slice(b * BLOCK, (b + 1) * BLOCK)
        wc[:BLOCK, rows] = wq_ref[rows, :].T
    for i in range(8):
        for half, b in enumerate(slice_blocks(i)):
            first = (2 * i + half) * BLOCK
            wot[first : first + BLOCK, :] = wo_ref[:, b * BLOCK : (b + 1) * BLOCK].T
    dkv_acc[...] = jnp.zeros_like(dkv_acc)

    @pl.when(s == SECTIONS - 1)
    def _():
        for k in range(CHUNKS):
            m, first = k % 2, (PARTS - 1 - k // 2) * ROWS
            for i in range(8):
                for half, b in enumerate(slice_blocks(i)):
                    g_buf[k, i, :, half * BLOCK : (half + 1) * BLOCK] = top_ref[
                        m, first : first + ROWS, b * BLOCK : (b + 1) * BLOCK
                    ]

    far_row = pl.multiple_of(BLOCK + ((1 - z_pos) * 2 + c_pos) * 64, 64)
    far_near_row = pl.multiple_of(BLOCK + ((1 - z_pos) * 2 + 1 - c_pos) * 64, 64)
    near_row = pl.multiple_of(BLOCK + (z_pos * 2 + 1 - c_pos) * 64, 64)
    kv_copy(far_row, peer(0, 1, 0), 1).wait_recv()

    @pl.when(s >= 4)
    def _():
        pl.semaphore_signal(gate, inc=1, device_id=(s - 4, d), device_id_type=MESH)

    far_near = kv_copy(far_row, peer(0, 0, 1), 2)
    far_near.start()
    kv_copy(near_row, peer(0, 0, 1), 0).wait_recv()
    kv_copy(far_near_row, peer(0, 0, 1), 2).wait_recv()
    own_near.wait_send()
    own_far.wait_send()
    far_near.wait_send()

    keyval = dot(normed[...], wc[BLOCK:, :], 1, 1)
    for i in range(CHUNKS):
        m, first = i % 2, (PARTS - 1 - i // 2) * ROWS
        part = keyval[i * ROWS : (i + 1) * ROWS, :]
        kv_hat[i] = part
        k_low[m, first : first + ROWS, :] = part[:, :HEAD_DIM].astype(BF16)
        v_low[m, first : first + ROWS, :] = part[:, HEAD_DIM:].astype(BF16)
    for i in range(CHUNKS):
        m, first = i % 2, (PARTS - 1 - i // 2) * ROWS
        scores = dot(q_low[i], k_low[m], 1, 1) * SCALE
        row = lax.rem(lax.broadcasted_iota(jnp.int32, scores.shape, 0), ROWS) + first
        scores = jnp.where(row >= lax.broadcasted_iota(jnp.int32, scores.shape, 1), scores, -1e30)
        scores = jnp.exp(scores - jnp.max(scores, axis=-1, keepdims=True))
        probs = scores / jnp.sum(scores, axis=-1, keepdims=True)
        p_buf[i] = probs
        low = probs.astype(BF16)
        p_low[i] = low
        attended = dot(low, v_low[m]).astype(BF16)
        for h in range(2):
            att[i, :, h * HEAD_DIM : (h + 1) * HEAD_DIM] = attended[h * ROWS : (h + 1) * ROWS, :]

    own_slice = x_pos * 2 + c_pos

    def ag_copy(k, offset):
        return pltpu.make_async_remote_copy(
            src_ref=ag_buf.at[k], dst_ref=g_buf.at[k, own_slice],
            send_sem=ag_send.at[k], recv_sem=ag_recv.at[k],
            device_id=(s - 1, peer(offset[0], 0, offset[1])), device_id_type=MESH,
        )

    def all_of(ref, sem):
        return pltpu.make_async_copy(ref, ref, sem)

    def first_half(k):
        m = k % 2
        first = pl.multiple_of((PARTS - 1 - k // 2) * ROWS, ROWS)

        @pl.when(s < SECTIONS - 1)
        def _():
            all_of(g_buf.at[k], ag_recv.at[k]).wait()

        g = jnp.concatenate([g_buf[k, i] for i in range(8)], axis=1)
        og = dot(g, wot[...]).astype(BF16)
        og = jnp.concatenate([og[:, :HEAD_DIM], og[:, HEAD_DIM:]], axis=0)
        prob_grad = dot(og, v_low[m], 1, 1)
        probs = p_buf[k]
        delta = jnp.sum(probs * prob_grad, axis=-1, keepdims=True)
        score_grad = (probs * (prob_grad - delta)).astype(BF16)
        dq = (dot(score_grad, k_low[m]) * SCALE).astype(BF16)
        dkv_acc[m, :, :HEAD_DIM] += dot(score_grad, q_low[k], 0, 0) * SCALE
        dkv_acc[m, :, HEAD_DIM:] += dot(p_low[k], og, 0, 0)
        dkv = dkv_acc[m, pl.ds(first, ROWS), :].astype(BF16)
        stat = jnp.sum(dq.astype(F32) * q_hat[k], axis=-1, keepdims=True)
        stat = stat[:ROWS] + stat[ROWS:]
        stat += jnp.sum(dkv.astype(F32) * kv_hat[k], axis=-1, keepdims=True)
        r = r_buf[k]
        stat = stat * (r * r / WIDTH)
        grads = jnp.concatenate([dq[:ROWS], dq[ROWS:], dkv], axis=1)
        for j, (dx, dc) in enumerate(SLICES):
            base = (x_pos + dx) % 4 * 4 + (c_pos + dc) % 2
            for half in range(2):
                block = columns(base + half * 2)
                part = dot(grads, wc[:, block])
                xb = x_ref[m, pl.ds(first, ROWS), block].astype(F32)
                part = part * (r * gain_ref[:, block]) - xb * stat
                part_buf[k, j, :, half * BLOCK : (half + 1) * BLOCK] = part.astype(BF16)
            for dz in (1, 0):
                if (dx, dz, dc) == (0, 0, 0):
                    continue
                pltpu.make_async_remote_copy(
                    src_ref=part_buf.at[k, j], dst_ref=rs_buf.at[k, PEERS.index((dx, dz, dc))],
                    send_sem=rs_send.at[k], recv_sem=rs_recv.at[k],
                    device_id=(s, peer(dx, dz, dc)), device_id_type=MESH,
                ).start()

    def second_half(k):
        m = k % 2
        first = pl.multiple_of((PARTS - 1 - k // 2) * ROWS, ROWS)
        total = g_buf[k, own_slice].astype(F32) + part_buf[k, len(SLICES) - 1].astype(F32)
        all_of(rs_buf.at[k], rs_recv.at[k]).wait()
        for j in range(len(PEERS)):
            total += rs_buf[k, j].astype(F32)
        result = total.astype(BF16)
        ag_buf[k] = result

        @pl.when(s > 0)
        def _():
            for offset in SLICES:
                ag_copy(k, offset).start()

        out_ref[m, pl.ds(first, ROWS), :] = jnp.where(
            z_pos == 0, result[:, :BLOCK], result[:, BLOCK:]
        )

    def grad_copy(i):
        part = pl.ds(i * 1024, 1024)
        return pltpu.make_async_copy(grad_buf.at[:, part], grad_ref.at[:, part], grad_sem.at[i])

    def weight_grad():
        attended = att[...].reshape(CHUNKS * ROWS, BLOCK)
        for i in range(8):
            g = g_buf[:, i].reshape(CHUNKS * ROWS, SLICE)
            part = dot(attended, g, 0, 0)
            for half, b in enumerate(slice_blocks(i)):
                grad_buf[:, b * BLOCK : (b + 1) * BLOCK] = part[:, half * BLOCK : (half + 1) * BLOCK]
            if i % 2 == 1:
                grad_copy(i // 2).start()

    grad_step = jnp.where(s == 0, CHUNKS, CHUNKS + LAG)

    def step(k, carry):
        @pl.when(k < CHUNKS)
        def _():
            first_half(k)

        @pl.when(k == grad_step)
        def _():
            weight_grad()

        @pl.when((k >= LAG) & (k < CHUNKS + LAG))
        def _():
            second_half(k - LAG)

        return carry

    lax.fori_loop(0, CHUNKS + LAG + 1, step, 0)

    for i in range(4):
        grad_copy(i).wait()

    def drain(k, carry):
        all_of(rs_buf.at[k], rs_send.at[k]).wait()

        @pl.when(s > 0)
        def _():
            all_of(g_buf.at[k], ag_send.at[k]).wait()

        return carry

    lax.fori_loop(0, CHUNKS, drain, 0)


def relay(x, top, wq, wkv, wo, gain):
    vmem = pl.BlockSpec(memory_space=pltpu.VMEM)
    return pl.pallas_call(
        kernel,
        out_shape=(
            jax.ShapeDtypeStruct((MICRO, TOKENS, BLOCK), BF16),
            jax.ShapeDtypeStruct((BLOCK, WIDTH), F32),
        ),
        in_specs=[vmem] * 6,
        out_specs=(vmem, pl.BlockSpec(memory_space=pl.ANY)),
        scratch_shapes=[
            pltpu.VMEM((2 * BLOCK, WIDTH), BF16),
            pltpu.VMEM((WIDTH, BLOCK), BF16),
            pltpu.VMEM((CHUNKS * ROWS, WIDTH), BF16),
            pltpu.VMEM((CHUNKS, ROWS, 1), F32),
            pltpu.VMEM((CHUNKS, 2 * ROWS, HEAD_DIM), F32),
            pltpu.VMEM((CHUNKS, 2 * ROWS, HEAD_DIM), BF16),
            pltpu.VMEM((CHUNKS, ROWS, BLOCK), F32),
            pltpu.VMEM((MICRO, TOKENS, HEAD_DIM), BF16),
            pltpu.VMEM((MICRO, TOKENS, HEAD_DIM), BF16),
            pltpu.VMEM((CHUNKS, 2 * ROWS, TOKENS), F32),
            pltpu.VMEM((CHUNKS, 2 * ROWS, TOKENS), BF16),
            pltpu.VMEM((CHUNKS, ROWS, BLOCK), BF16),
            pltpu.VMEM((MICRO, TOKENS, BLOCK), F32),
            pltpu.VMEM((CHUNKS, 8, ROWS, SLICE), BF16),
            pltpu.VMEM((CHUNKS, 8, ROWS, SLICE), BF16),
            pltpu.VMEM((CHUNKS, len(PEERS), ROWS, SLICE), BF16),
            pltpu.VMEM((CHUNKS, ROWS, SLICE), BF16),
            pltpu.VMEM((BLOCK, WIDTH), F32),
            pltpu.SemaphoreType.DMA((CHUNKS,)),
            pltpu.SemaphoreType.DMA((CHUNKS,)),
            pltpu.SemaphoreType.DMA((CHUNKS,)),
            pltpu.SemaphoreType.DMA((CHUNKS,)),
            pltpu.SemaphoreType.DMA((3,)),
            pltpu.SemaphoreType.DMA((3,)),
            pltpu.SemaphoreType.DMA((4,)),
            pltpu.SemaphoreType.REGULAR,
        ],
        compiler_params=pltpu.CompilerParams(
            collective_id=0, has_side_effects=True, vmem_limit_bytes=48 * 1024 * 1024
        ),
        name="relay",
    )(x, top, wq, wkv, wo, gain)


def body(layer_inputs, top_grad, w_query, w_keyval, w_out, norm_gain, new_block):
    stream, grad = relay(
        layer_inputs[0], top_grad, w_query[0], w_keyval[0], w_out[0], norm_gain.astype(F32)
    )
    return stream[None], (grad * new_block[0].astype(F32))[None]


def solution(mesh):
    in_specs = (
        P("section", None, None, None),
        P(),
        P("section", None, "dp"),
        P("section", None, "dp"),
        P("section", "dp", None),
        P("section", None),
        P("section"),
    )
    out_specs = (P("section", None, None, "dp"), P("section", "dp", None))
    return jax.shard_map(body, mesh=mesh, in_specs=in_specs, out_specs=out_specs, check_vma=False)
```

time: 2380 us -> 379 us (0.16)
  waiting for transfers between devices: 1470 us -> 0 us
  blocking collectives: 531 us -> 0 us
  Pallas kernels: 0 us -> 366 us
  matrix products: 239 us -> 0 us
  other arithmetic: 75.6 us -> 5.37 us
  starting transfers between devices: 30.6 us -> 0 us
    reduce_scatter x17 -> x0, waiting for transfers between devices: 1290 us -> none  [backward_step(): lax.psum_scatter(partial_value.astype(jnp.bfloat16), 'dp', scatter_dimens...]
    all_gather x17 -> x0, blocking collectives: 531 us -> none  [tick_whole(): lax.all_gather(norm_part, 'dp', axis=1, tiled=True).astype(jnp.float32)]
    pallas_call x0 -> x1, Pallas kernels: none -> 366 us  [relay(): pl.pallas_call(kernel, out_shape=(jax.ShapeDtypeStruct((MICRO, TOKENS, BL...]
    dot_general x187 -> x0, matrix products: 235 us -> none  [the longest x17 81.8 us: layer_terms(): jnp.einsum('tk,tc->kc', attended_flat, upstream, preferred_element_type=j...]
    ppermute x19 -> x0, waiting for transfers between devices: 186 us -> none  [the longest x17 155 us: shifted(): return lax.ppermute(value, axis, pairs)]
    reduce_sum x34 -> x0, other arithmetic: 46 us -> none  [the longest x17 23.7 us: layer_terms(): jnp.mean(inputs_f * inputs_f, axis=-1, keepdims=True) + EPS]
    ppermute x19 -> x0, starting transfers between devices: 30.6 us -> none  [the longest x17 22 us: shifted(): return lax.ppermute(value, axis, pairs)]
    convert_element_type x35 -> x1, other arithmetic: 24.7 us -> 0.74 us  [body(): norm_gain.astype(F32)]
  transfers between devices with their start and end apart: 36 -> 0, of which waited for: 36 -> 0; matrix products, arithmetic and copies ran while one was open for 4% -> 0% of each run, Pallas kernels for 0% -> 0%
where the time goes in v1:
time: 379 us
  Pallas kernels  366 us (97%)
  local copies, waits for them, and re-layouts  6.18 us (2%)
  other arithmetic  5.37 us (1%)
    pallas_call x1, Pallas kernels, relay(): pl.pallas_call(kernel, out_shape=(jax.ShapeDtypeStruct((MICRO, TOKENS, BL...  366 us

profile of v1, /device:TPU:1, one launch (start us, length us, event | category | flops | bytes accessed | tf_op | source)
XLA Modules:
  0.0 378.6 jit_solution(9870694617175664549)
XLA Ops:
  1.3 0.7 convert_element_type.9.gain_ref
  2.0 1.5 copy.9
  3.5 0.0 copy-start
  3.6 1.6 copy-done
  5.1 0.0 copy-start.1
  5.1 1.2 copy-done.1
  6.4 0.0 copy-start.2
  6.4 1.2 copy-done.2
  7.6 365.7 %relay.1 = (bf16[2,64,256]{2,1,0:T(8,128)(2,1)S(1)}, f32[256,4096]{1,0:T(8,128)}) custom-call(bf16[2,64,4096]{2,1,0:T(8,128)(2,1)S(1)} %bitcast.10, bf16[2,64,4096]{2,1,0:T(8,128)(2,1)S(1)} %copy-done.2, bf16[4096,256]{1,0:T(8,128)(2,1)S(1)} %bitcast.9, bf16[4096,64]{1,0:T(8,128)(2,1)S(1)} %bitcast.8, bf16[256,4096]{1,0:T(8,128)(2,1)} %bitcast.12, ...), custom_call_target="tpu_custom_call" | custom-call | tf_op jit(solution)/shard_map/relay/pallas_call | solution.py:303
  373.3 4.6 %multiply_bitcast_fusion = f32[1,256,4096]{2,1,0:T(8,128)} fusion(f32[256,4096]{1,0:T(8,128)} %get-tuple-element.5, f32[]{:T(128)} %bitcast.5), kind=kLoop, calls=%fused_computation | loop fusion | flops 1048576 | bytes 8388612 | tf_op jit(solution)/shard_map/broadcast_in_dim | solution.py:350
  377.9 0.6 copy.12
Async XLA Ops:
  3.5 1.6 copy-start
  5.1 1.2 copy-start.1
  6.4 1.2 copy-start.2

commit v2 on v1

v2 whole, which is shorter than its diff:
```python
import jax
import jax.numpy as jnp
from jax import lax
from jax.experimental import pallas as pl
from jax.experimental.pallas import tpu as pltpu
from jax.sharding import PartitionSpec as P

HEAD_DIM = 128
EPS = 1e-05
MESH = pl.DeviceIdType.MESH
F32 = jnp.float32
BF16 = jnp.bfloat16

SECTIONS = 16
TOKENS = 64
MICRO = 2
WIDTH = 4096
ROWS = 16
PARTS = TOKENS // ROWS
CHUNKS = MICRO * PARTS
LAG = 1
BLOCK = 256
SLICE = 2 * BLOCK
SCALE = HEAD_DIM ** (-0.5)

HOPS = (2, 1, 3, 0)
PEERS = [(dx, dz) for dx in HOPS for dz in (1, 0)][:-1]
PIECES = 4


def dot(a, b, ca=1, cb=0):
    return lax.dot_general(a, b, (((ca,), (cb,)), ((), ())), preferred_element_type=F32)


def columns(block):
    return pl.ds(pl.multiple_of(block * BLOCK, BLOCK), BLOCK)


def slice_blocks(index):
    return [(index // 2) * 4 + half * 2 + index % 2 for half in range(2)]


def place(k):
    return k % 2, (PARTS - 1 - k // 2) * ROWS


def kernel(
    x_hbm, top_hbm, wq_hbm, wkv_hbm, wo_hbm, gain_ref,
    out_ref, att, g_out,
    x_ref, top_ref, wq_ref, wo_ref,
    wc, wot, normed, r_buf, q_hat, q_low, kvt, k_t, v_t, k_low, v_low, p_buf, p_low_t, dkv_acc,
    g_buf, near_out, near_in, part_buf, rs_buf, ag_buf,
    load_sem, near_send, near_recv, rs_send, rs_recv, ag_send, ag_recv,
    kv_send, kv_recv, far_send, far_recv, pass_send, pass_recv, gate,
):
    s = lax.axis_index("section")
    d = lax.axis_index("dp")
    x_pos = d // 4
    z_pos = d // 2 % 2
    c_pos = d % 2
    top_section = s == SECTIONS - 1

    def peer(dx, dz, dc):
        return (x_pos + dx) % 4 * 4 + (z_pos + dz) % 2 * 2 + (c_pos + dc) % 2

    def all_of(ref, sem):
        return pltpu.make_async_copy(ref, ref, sem)

    def remote(src, dst, send, recv, section, device):
        return pltpu.make_async_remote_copy(
            src_ref=src, dst_ref=dst, send_sem=send, recv_sem=recv,
            device_id=(section, device), device_id_type=MESH,
        )

    own_row = pl.multiple_of((z_pos * 2 + c_pos) * 64, 64)
    near_row = pl.multiple_of((z_pos * 2 + 1 - c_pos) * 64, 64)
    far_row = pl.multiple_of(((1 - z_pos) * 2 + c_pos) * 64, 64)
    cross_row = pl.multiple_of(((1 - z_pos) * 2 + 1 - c_pos) * 64, 64)

    def wc_rows(row):
        return wc.at[pl.ds(pl.multiple_of(BLOCK + row, 64), 64)]

    load_x = pltpu.make_async_copy(x_hbm, x_ref, load_sem.at[0])
    load_kv = pltpu.make_async_copy(wkv_hbm, wc_rows(own_row), load_sem.at[1])
    load_q = pltpu.make_async_copy(wq_hbm, wq_ref, load_sem.at[2])
    load_o = pltpu.make_async_copy(wo_hbm, wo_ref, load_sem.at[3])
    load_top = pltpu.make_async_copy(top_hbm, top_ref, load_sem.at[4])
    for load in (load_x, load_kv, load_q, load_o):
        load.start()

    @pl.when(top_section)
    def _():
        load_top.start()

    barrier = pltpu.get_barrier_semaphore()

    def greet(section, device):
        pl.semaphore_signal(barrier, inc=1, device_id=(section, device), device_id_type=MESH)

    for dx, dz in PEERS:
        greet(s, peer(dx, dz, 0))
    greet(s, peer(0, 0, 1))
    greet(s, peer(0, 1, 1))

    @pl.when(s > 0)
    def _():
        for dx in HOPS:
            for dc in range(2):
                greet(s - 1, peer(dx, 0, dc))

    @pl.when(s < SECTIONS - 1)
    def _():
        for dx in HOPS:
            for dc in range(2):
                greet(s + 1, peer(dx, 0, dc))

    @pl.when(s < SECTIONS - 4)
    def _():
        greet(s + 4, d)

    load_x.wait()
    for m in range(MICRO):
        for first in range(0, TOKENS, ROWS):
            xf = x_ref[m, first : first + ROWS, :].astype(F32)
            r = lax.rsqrt(jnp.mean(xf * xf, axis=-1, keepdims=True) + EPS)
            r_buf[m, first : first + ROWS, :] = r
            rows = slice(m * TOKENS + first, m * TOKENS + first + ROWS)
            normed[rows, :] = (xf * r * gain_ref[...].astype(F32)).astype(BF16)
    load_kv.wait()
    kvt[pl.ds(own_row, 64), :] = dot(wc[pl.ds(BLOCK + own_row, 64), :], normed[...], 1, 1).astype(BF16)

    greetings = (
        len(PEERS) + 2
        + jnp.where(s > 0, 8, 0)
        + jnp.where(s < SECTIONS - 1, 8, 0)
        + jnp.where(s >= 4, 1, 0)
    )
    pl.semaphore_wait(barrier, greetings)

    own_kvt = kvt.at[pl.ds(own_row, 64)]
    kvt_copies = [
        remote(own_kvt, own_kvt, kv_send.at[i], kv_recv.at[i], s, peer(0, dz, dc))
        for i, (dz, dc) in enumerate([(1, 0), (1, 1), (0, 1)])
    ]
    for copy in kvt_copies:
        copy.start()

    def piece(row, i):
        width = WIDTH // PIECES
        return wc.at[pl.ds(pl.multiple_of(BLOCK + row, 64), 64), pl.ds(i * width, width)]

    def across(row, i):
        part = piece(row, i)
        return remote(part, part, far_send.at[i], far_recv.at[i], s, peer(0, 1, 0))

    def beside(row, i, sem):
        part = piece(row, i)
        return remote(part, part, pass_send.at[sem], pass_recv.at[sem], s, peer(0, 0, 1))

    @pl.when(s >= SECTIONS - 4)
    def _():
        for i in range(PIECES):
            across(own_row, i).start()

    for i in range(PIECES):
        beside(own_row, i, i).start()

    load_q.wait()
    queries = dot(normed[...], wq_ref[...])
    for k in range(CHUNKS):
        m, first = place(k)
        rows = slice(m * TOKENS + first, m * TOKENS + first + ROWS)
        for h in range(2):
            part = queries[rows, h * HEAD_DIM : (h + 1) * HEAD_DIM]
            q_hat[k, h * ROWS : (h + 1) * ROWS, :] = part
            q_low[k, h * ROWS : (h + 1) * ROWS, :] = part.astype(BF16)
    for b in range(WIDTH // BLOCK):
        rows = slice(b * BLOCK, (b + 1) * BLOCK)
        wc[:BLOCK, rows] = wq_ref[rows, :].T
    load_o.wait()
    for i in range(8):
        for half, b in enumerate(slice_blocks(i)):
            first = (2 * i + half) * BLOCK
            wot[first : first + BLOCK, :] = wo_ref[:, b * BLOCK : (b + 1) * BLOCK].T
    dkv_acc[...] = jnp.zeros_like(dkv_acc)

    @pl.when(top_section)
    def _():
        load_top.wait()
        for k in range(CHUNKS):
            m, first = place(k)
            for i in range(8):
                for half, b in enumerate(slice_blocks(i)):
                    g_buf[k, i, :, half * BLOCK : (half + 1) * BLOCK] = top_ref[
                        m, first : first + ROWS, b * BLOCK : (b + 1) * BLOCK
                    ]

    for copy in kvt_copies:
        copy.wait_recv()
    keyval = kvt[...].T
    for m in range(MICRO):
        rows = slice(m * TOKENS, (m + 1) * TOKENS)
        k_t[m] = kvt[:HEAD_DIM, rows]
        v_t[m] = kvt[HEAD_DIM:, rows]
        k_low[m] = keyval[rows, :HEAD_DIM]
        v_low[m] = keyval[rows, HEAD_DIM:]
    for k in range(CHUNKS):
        m, first = place(k)
        scores = dot(q_low[k], k_t[m]) * SCALE
        row = lax.rem(lax.broadcasted_iota(jnp.int32, scores.shape, 0), ROWS) + first
        scores = jnp.where(row >= lax.broadcasted_iota(jnp.int32, scores.shape, 1), scores, -1e30)
        scores = jnp.exp(scores - jnp.max(scores, axis=-1, keepdims=True))
        probs = scores / jnp.sum(scores, axis=-1, keepdims=True)
        p_buf[k] = probs
        p_low_t[k] = probs.T.astype(BF16)
        attended = dot(probs.astype(BF16), v_low[m]).astype(BF16)
        for h in range(2):
            att[k, :, h * HEAD_DIM : (h + 1) * HEAD_DIM] = attended[h * ROWS : (h + 1) * ROWS, :]

    @pl.when(s < SECTIONS - 4)
    def _():
        pl.semaphore_wait(gate, 1)
        for i in range(PIECES):
            across(own_row, i).start()

    for i in range(PIECES):
        across(far_row, i).wait_recv()
        beside(far_row, i, PIECES + i).start()

    @pl.when(s >= 4)
    def _():
        pl.semaphore_signal(gate, inc=1, device_id=(s - 4, d), device_id_type=MESH)

    for i in range(PIECES):
        beside(near_row, i, i).wait_recv()
        beside(cross_row, i, PIECES + i).wait_recv()

    own_slice = x_pos * 2 + c_pos

    def ag_copy(k, dx, dc):
        return remote(
            ag_buf.at[k], g_buf.at[k, own_slice], ag_send.at[k], ag_recv.at[k],
            s - 1, peer(dx, 0, dc),
        )

    def first_half(k):
        m, first = place(k)
        first = pl.multiple_of(first, ROWS)

        @pl.when(s < SECTIONS - 1)
        def _():
            all_of(g_buf.at[k], ag_recv.at[k]).wait()

        g = jnp.concatenate([g_buf[k, i] for i in range(8)], axis=1)
        og = dot(g, wot[...]).astype(BF16)
        og = jnp.concatenate([og[:, :HEAD_DIM], og[:, HEAD_DIM:]], axis=0)
        prob_grad = dot(og, v_t[m])
        probs = p_buf[k]
        delta = jnp.sum(probs * prob_grad, axis=-1, keepdims=True)
        score_grad = (probs * (prob_grad - delta)).astype(BF16)
        dq = (dot(score_grad, k_low[m]) * SCALE).astype(BF16)
        dkv_acc[m, :, :HEAD_DIM] += dot(score_grad, q_low[k], 0, 0) * SCALE
        dkv_acc[m, :, HEAD_DIM:] += dot(p_low_t[k], og)
        dkv = dkv_acc[m, pl.ds(first, ROWS), :].astype(BF16)
        keyval = jnp.concatenate(
            [k_low[m, pl.ds(first, ROWS), :], v_low[m, pl.ds(first, ROWS), :]], axis=1
        )
        stat = jnp.sum(dq.astype(F32) * q_hat[k], axis=-1, keepdims=True)
        stat = stat[:ROWS] + stat[ROWS:]
        stat += jnp.sum(dkv.astype(F32) * keyval.astype(F32), axis=-1, keepdims=True)
        r = r_buf[m, pl.ds(first, ROWS), :]
        stat = stat * (r * r / WIDTH)
        grads = jnp.concatenate([dq[:ROWS], dq[ROWS:], dkv], axis=1)

        def contribution(dx, dc):
            parts = []
            for half in range(2):
                block = columns((x_pos + dx) % 4 * 4 + half * 2 + (c_pos + dc) % 2)
                part = dot(grads, wc[:, block]) * (r * gain_ref[:, block].astype(F32))
                parts.append(part - x_ref[m, pl.ds(first, ROWS), block].astype(F32) * stat)
            return jnp.concatenate(parts, axis=1)

        for j, dx in enumerate(HOPS):
            near_out[k, j] = contribution(dx, 1).astype(BF16)
            remote(
                near_out.at[k, j], near_in.at[k, j], near_send.at[k], near_recv.at[k, j],
                s, peer(0, 0, 1),
            ).start()
        own = [contribution(dx, 0) for dx in HOPS]
        g_out[k] = g_buf[k]
        for j, dx in enumerate(HOPS):
            all_of(near_in.at[k, j], near_recv.at[k, j]).wait()
            part_buf[k, j] = (own[j] + near_in[k, j].astype(F32)).astype(BF16)
            for dz in (1, 0):
                if (dx, dz) == (0, 0):
                    continue
                remote(
                    part_buf.at[k, j], rs_buf.at[k, PEERS.index((dx, dz))],
                    rs_send.at[k], rs_recv.at[k], s, peer(dx, dz, 0),
                ).start()

    def second_half(k):
        m, first = place(k)
        first = pl.multiple_of(first, ROWS)
        total = g_buf[k, own_slice].astype(F32) + part_buf[k, len(HOPS) - 1].astype(F32)
        all_of(rs_buf.at[k], rs_recv.at[k]).wait()
        for j in range(len(PEERS)):
            total += rs_buf[k, j].astype(F32)
        result = total.astype(BF16)
        ag_buf[k] = result

        @pl.when(s > 0)
        def _():
            for dx in HOPS:
                for dc in (1, 0):
                    ag_copy(k, dx, dc).start()

        out_ref[m, pl.ds(first, ROWS), :] = jnp.where(
            z_pos == 0, result[:, :BLOCK], result[:, BLOCK:]
        )

    def step(k, carry):
        @pl.when(k < CHUNKS)
        def _():
            first_half(k)

        @pl.when(k >= LAG)
        def _():
            second_half(k - LAG)

        return carry

    lax.fori_loop(0, CHUNKS + LAG, step, 0)

    for copy in kvt_copies:
        copy.wait_send()
    for i in range(PIECES):
        across(own_row, i).wait_send()
        beside(own_row, i, i).wait_send()
        beside(far_row, i, PIECES + i).wait_send()

    def drain(k, carry):
        all_of(near_in.at[k], near_send.at[k]).wait()
        all_of(rs_buf.at[k], rs_send.at[k]).wait()

        @pl.when(s > 0)
        def _():
            all_of(g_buf.at[k], ag_send.at[k]).wait()

        return carry

    lax.fori_loop(0, CHUNKS, drain, 0)


def relay(x, top, wq, wkv, wo, gain):
    vmem = pl.BlockSpec(memory_space=pltpu.VMEM)
    hbm = pl.BlockSpec(memory_space=pl.ANY)
    dma = pltpu.SemaphoreType.DMA
    return pl.pallas_call(
        kernel,
        out_shape=(
            jax.ShapeDtypeStruct((MICRO, TOKENS, BLOCK), BF16),
            jax.ShapeDtypeStruct((CHUNKS, ROWS, BLOCK), BF16),
            jax.ShapeDtypeStruct((CHUNKS, 8, ROWS, SLICE), BF16),
        ),
        in_specs=[hbm] * 5 + [vmem],
        out_specs=(vmem, vmem, vmem),
        scratch_shapes=[
            pltpu.VMEM((MICRO, TOKENS, WIDTH), BF16),
            pltpu.VMEM((MICRO, TOKENS, WIDTH), BF16),
            pltpu.VMEM((WIDTH, BLOCK), BF16),
            pltpu.VMEM((BLOCK, WIDTH), BF16),
            pltpu.VMEM((2 * BLOCK, WIDTH), BF16),
            pltpu.VMEM((WIDTH, BLOCK), BF16),
            pltpu.VMEM((MICRO * TOKENS, WIDTH), BF16),
            pltpu.VMEM((MICRO, TOKENS, 1), F32),
            pltpu.VMEM((CHUNKS, 2 * ROWS, HEAD_DIM), F32),
            pltpu.VMEM((CHUNKS, 2 * ROWS, HEAD_DIM), BF16),
            pltpu.VMEM((BLOCK, MICRO * TOKENS), BF16),
            pltpu.VMEM((MICRO, HEAD_DIM, TOKENS), BF16),
            pltpu.VMEM((MICRO, HEAD_DIM, TOKENS), BF16),
            pltpu.VMEM((MICRO, TOKENS, HEAD_DIM), BF16),
            pltpu.VMEM((MICRO, TOKENS, HEAD_DIM), BF16),
            pltpu.VMEM((CHUNKS, 2 * ROWS, TOKENS), F32),
            pltpu.VMEM((CHUNKS, TOKENS, 2 * ROWS), BF16),
            pltpu.VMEM((MICRO, TOKENS, BLOCK), F32),
            pltpu.VMEM((CHUNKS, 8, ROWS, SLICE), BF16),
            pltpu.VMEM((CHUNKS, len(HOPS), ROWS, SLICE), BF16),
            pltpu.VMEM((CHUNKS, len(HOPS), ROWS, SLICE), BF16),
            pltpu.VMEM((CHUNKS, len(HOPS), ROWS, SLICE), BF16),
            pltpu.VMEM((CHUNKS, len(PEERS), ROWS, SLICE), BF16),
            pltpu.VMEM((CHUNKS, ROWS, SLICE), BF16),
            dma((5,)),
            dma((CHUNKS,)),
            dma((CHUNKS, len(HOPS))),
            dma((CHUNKS,)),
            dma((CHUNKS,)),
            dma((CHUNKS,)),
            dma((CHUNKS,)),
            dma((3,)),
            dma((3,)),
            dma((PIECES,)),
            dma((PIECES,)),
            dma((2 * PIECES,)),
            dma((2 * PIECES,)),
            pltpu.SemaphoreType.REGULAR,
        ],
        compiler_params=pltpu.CompilerParams(
            collective_id=0, has_side_effects=True, vmem_limit_bytes=60 * 1024 * 1024
        ),
        name="relay",
    )(x, top, wq, wkv, wo, gain)


def weight_kernel(block_ref, att_ref, g_ref, grad_ref):
    attended = att_ref[...].reshape(CHUNKS * ROWS, BLOCK)
    scale = block_ref[0].astype(F32)
    for core in range(2):
        g = g_ref[:, core].reshape(CHUNKS * ROWS, SLICE)
        part = dot(attended, g, 0, 0) * scale
        for half in range(2):
            first = (half * 2 + core) * BLOCK
            grad_ref[:, first : first + BLOCK] = part[:, half * BLOCK : (half + 1) * BLOCK]


def weight_grad(new_block, att, g):
    return pl.pallas_call(
        weight_kernel,
        out_shape=jax.ShapeDtypeStruct((BLOCK, WIDTH), F32),
        grid=(4,),
        in_specs=[
            pl.BlockSpec(memory_space=pltpu.SMEM),
            pl.BlockSpec((CHUNKS, ROWS, BLOCK), lambda i: (0, 0, 0)),
            pl.BlockSpec((CHUNKS, 2, ROWS, SLICE), lambda i: (0, i, 0, 0)),
        ],
        out_specs=pl.BlockSpec((BLOCK, 4 * BLOCK), lambda i: (0, i)),
        compiler_params=pltpu.CompilerParams(vmem_limit_bytes=16 * 1024 * 1024),
        name="weight_grad",
    )(new_block, att, g)


def body(layer_inputs, top_grad, w_query, w_keyval, w_out, norm_gain, new_block):
    stream, att, g = relay(
        layer_inputs[0], top_grad, w_query[0], w_keyval[0].T, w_out[0], norm_gain
    )
    return stream[None], weight_grad(new_block, att, g)[None]


def solution(mesh):
    in_specs = (
        P("section", None, None, None),
        P(),
        P("section", None, "dp"),
        P("section", None, "dp"),
        P("section", "dp", None),
        P("section", None),
        P("section"),
    )
    out_specs = (P("section", None, None, "dp"), P("section", "dp", None))
    return jax.shard_map(body, mesh=mesh, in_specs=in_specs, out_specs=out_specs, check_vma=False)
```

time: 379 us -> 293 us (0.77)
  Pallas kernels: 366 us -> 288 us
  other arithmetic: 5.37 us -> 0 us
    pallas_call x1, Pallas kernels: 366 us -> 285 us  [relay(): pl.pallas_call(kernel, out_shape=(jax.ShapeDtypeStruct((MICRO, TOKENS, BL...]
    broadcast_in_dim x1 -> x0, other arithmetic: 4.63 us -> none  [body(): return (stream[None], (grad * new_block[0].astype(F32))[None])]
where the time goes in v2:
time: 293 us; the launch traced here: 292 us
  Pallas kernels  288 us (98%)
    pallas_call x1, Pallas kernels, relay(): pl.pallas_call(kernel, out_shape=(jax.ShapeDtypeStruct((MICRO, TOKENS, BL...  285 us

profile of v2, /device:TPU:1, one launch (start us, length us, event | category | flops | bytes accessed | tf_op | source)
XLA Modules:
  0.0 292.4 jit_solution(8681534248499686317)
XLA Ops:
  1.3 285.4 %relay.1 = (bf16[2,64,256]{2,1,0:T(8,128)(2,1)}, bf16[8,16,256]{2,1,0:T(8,128)(2,1)}, bf16[8,8,16,512]{3,2,1,0:T(8,128)(2,1)}) custom-call(bf16[2,64,4096]{2,1,0:T(8,128)(2,1)} %bitcast.11, bf16[2,64,4096]{2,1,0:T(8,128)(2,1)} %top_hbm.1, bf16[4096,256]{1,0:T(8,128)(2,1)} %bitcast.9, bf16[64,4096]{1,0:T(8,128)(2,1)} %bitcast.12, bf16[256,4096]{1,0:T(8,128)(2,1)} %bitcast.10, ...), custom_call_target="tpu_custom_call" | custom-call | tf_op jit(solution)/shard_map/relay/pallas_call | solution.py:359
  286.7 0.0 copy-start
  286.7 1.2 copy-done
  287.9 0.0 copy-start.1
  287.9 0.8 copy-done.1
  288.8 0.0 copy-start.2
  288.8 3.0 %weight_grad.1 = f32[256,4096]{1,0:T(8,128)} custom-call(s32[1]{0:T(128)S(6)} %copy.10.block_ref, bf16[8,16,256]{2,1,0:T(8,128)(2,1)S(1)} %copy-done.1, bf16[8,8,16,512]{3,2,1,0:T(8,128)(2,1)S(1)} %copy-done), custom_call_target="tpu_custom_call" | custom-call | tf_op jit(solution)/shard_map/weight_grad/pallas_call | solution.py:427
  291.8 0.0 copy-done.2
  291.8 0.6 copy.11
Async XLA Ops:
  286.7 1.2 copy-start
  287.9 0.8 copy-start.1
  288.8 3.0 %copy-start.2 = (bf16[2,64,256]{2,1,0:T(8,128)(2,1)S(1)}, bf16[2,64,256]{2,1,0:T(8,128)(2,1)}, u32[]{:S(2)}) copy-start(bf16[2,64,256]{2,1,0:T(8,128)(2,1)} %get-tuple-element.5) | copy-start | bytes 196612

commit v3 on v2

v3 whole, which is shorter than its diff:
```python
import jax
import jax.numpy as jnp
from jax import lax
from jax.experimental import pallas as pl
from jax.experimental.pallas import tpu as pltpu
from jax.sharding import PartitionSpec as P

HEAD_DIM = 128
EPS = 1e-05
MESH = pl.DeviceIdType.MESH
F32 = jnp.float32
BF16 = jnp.bfloat16

SECTIONS = 16
TOKENS = 64
MICRO = 2
WIDTH = 4096
ROWS = 16
PARTS = TOKENS // ROWS
CHUNKS = PARTS
LAG = 1
BLOCK = 256
SLICE = 4 * BLOCK
HEADS = 4
KV_ROW = HEADS * HEAD_DIM
SCALE = HEAD_DIM ** (-0.5)

HOPS = (2, 1, 3, 0)
PEERS = [(dx, dz) for dx in HOPS for dz in (1, 0)][:-1]
PIECES = 8


def dot(a, b, ca=1, cb=0):
    return lax.dot_general(a, b, (((ca,), (cb,)), ((), ())), preferred_element_type=F32)


def first_token(k):
    return (PARTS - 1 - k) * ROWS


def heads_to_rows(value):
    return jnp.concatenate(
        [value[:, h * HEAD_DIM : (h + 1) * HEAD_DIM] for h in range(HEADS)], axis=0
    )


def rows_to_heads(value):
    return jnp.concatenate([value[h * ROWS : (h + 1) * ROWS] for h in range(HEADS)], axis=1)


def kernel(
    x_hbm, top_hbm, wq_hbm, wkv_hbm, wo_hbm, gain_ref,
    out_ref, att_out, g_out,
    x_ref, top_ref, wq_ref, wo_ref,
    wc, wot, normed, r_buf, q_hat, q_low, kvt, k_t, v_t, k_low, v_low, p_buf, p_low_t, dkv_acc,
    g_buf, g_in, att_own, att_send, att_in, part_buf, rs_buf, ag_buf, side_buf, side_in,
    load_sem, rs_send, rs_recv, ag_send, ag_recv, w_send, w_recv, g_send, g_recv,
    side_send, side_recv, att_sem, kv_send, kv_recv, far_send, far_recv, pass_send, pass_recv, gate,
):
    s = lax.axis_index("section")
    d = lax.axis_index("dp")
    x_pos = d // 4
    z_pos = d // 2 % 2
    c_pos = d % 2
    other = 1 - c_pos
    top_section = s == SECTIONS - 1

    def peer(dx, dz, dc):
        return (x_pos + dx) % 4 * 4 + (z_pos + dz) % 2 * 2 + (c_pos + dc) % 2

    def all_of(ref, sem):
        return pltpu.make_async_copy(ref, ref, sem)

    def remote(src, dst, send, recv, section, device):
        return pltpu.make_async_remote_copy(
            src_ref=src, dst_ref=dst, send_sem=send, recv_sem=recv,
            device_id=(section, device), device_id_type=MESH,
        )

    own_row = pl.multiple_of((z_pos * 2 + c_pos) * 64, 64)
    near_row = pl.multiple_of((z_pos * 2 + 1 - c_pos) * 64, 64)
    far_row = pl.multiple_of(((1 - z_pos) * 2 + c_pos) * 64, 64)
    cross_row = pl.multiple_of(((1 - z_pos) * 2 + 1 - c_pos) * 64, 64)

    def wc_rows(row):
        return wc.at[pl.ds(pl.multiple_of(KV_ROW + row, 64), 64)]

    load_x = pltpu.make_async_copy(x_hbm, x_ref, load_sem.at[0])
    load_kv = pltpu.make_async_copy(wkv_hbm, wc_rows(own_row), load_sem.at[1])
    load_q = pltpu.make_async_copy(wq_hbm, wq_ref.at[c_pos], load_sem.at[2])
    load_o = pltpu.make_async_copy(wo_hbm, wo_ref.at[c_pos], load_sem.at[3])
    load_top = pltpu.make_async_copy(top_hbm, top_ref, load_sem.at[4])
    for load in (load_kv, load_x, load_q, load_o):
        load.start()

    @pl.when(top_section)
    def _():
        load_top.start()

    barrier = pltpu.get_barrier_semaphore()

    def greet(section, device):
        pl.semaphore_signal(barrier, inc=1, device_id=(section, device), device_id_type=MESH)

    for dx, dz in PEERS:
        greet(s, peer(dx, dz, 0))
    greet(s, peer(0, 0, 1))
    greet(s, peer(0, 1, 1))

    @pl.when(s > 0)
    def _():
        for dx in HOPS:
            greet(s - 1, peer(dx, 0, 0))

    @pl.when(s < SECTIONS - 1)
    def _():
        for dx in HOPS:
            greet(s + 1, peer(dx, 0, 0))

    @pl.when(s < SECTIONS - 4)
    def _():
        greet(s + 4, d)

    greetings = (
        len(PEERS) + 2
        + jnp.where(s > 0, len(HOPS), 0)
        + jnp.where(s < SECTIONS - 1, len(HOPS), 0)
        + jnp.where(s >= 4, 1, 0)
    )
    pl.semaphore_wait(barrier, greetings)
    load_kv.wait()

    def piece(row, i):
        width = WIDTH // PIECES
        return wc.at[pl.ds(pl.multiple_of(KV_ROW + row, 64), 64), pl.ds(i * width, width)]

    def across(row, i):
        part = piece(row, i)
        return remote(part, part, far_send.at[i], far_recv.at[i], s, peer(0, 1, 0))

    def beside(row, i, sem):
        part = piece(row, i)
        return remote(part, part, pass_send.at[sem], pass_recv.at[sem], s, peer(0, 0, 1))

    @pl.when(s >= SECTIONS - 4)
    def _():
        for i in range(PIECES):
            across(own_row, i).start()

    share_q = remote(wq_hbm, wq_ref.at[c_pos], w_send.at[0], w_recv.at[0], s, peer(0, 0, 1))
    share_o = remote(wo_hbm, wo_ref.at[c_pos], w_send.at[1], w_recv.at[1], s, peer(0, 0, 1))
    share_q.start()
    share_o.start()
    for i in range(PIECES):
        beside(own_row, i, i).start()

    load_x.wait()
    for m in range(MICRO):
        for first in range(0, TOKENS, ROWS):
            xf = x_ref[m, first : first + ROWS, :].astype(F32)
            r = lax.rsqrt(jnp.mean(xf * xf, axis=-1, keepdims=True) + EPS)
            r_buf[m, first : first + ROWS, :] = r
            normed[m, first : first + ROWS, :] = (xf * r * gain_ref[...].astype(F32)).astype(BF16)
    tokens = normed[...].reshape(MICRO * TOKENS, WIDTH)
    kvt[pl.ds(own_row, 64), :] = dot(wc[pl.ds(KV_ROW + own_row, 64), :], tokens, 1, 1).astype(BF16)

    own_kvt = kvt.at[pl.ds(own_row, 64)]
    kvt_copies = [
        remote(own_kvt, own_kvt, kv_send.at[i], kv_recv.at[i], s, peer(0, dz, dc))
        for i, (dz, dc) in enumerate([(1, 0), (1, 1), (0, 1)])
    ]
    for copy in kvt_copies:
        copy.start()

    load_q.wait()
    share_q.wait_recv()
    for half in range(2):
        queries = dot(normed[c_pos], wq_ref[half])
        for k in range(CHUNKS):
            first = first_token(k)
            for h in range(2):
                part = queries[first : first + ROWS, h * HEAD_DIM : (h + 1) * HEAD_DIM]
                row = (2 * half + h) * ROWS
                q_hat[k, row : row + ROWS, :] = part
                q_low[k, row : row + ROWS, :] = part.astype(BF16)
        for b in range(WIDTH // BLOCK):
            rows = slice(b * BLOCK, (b + 1) * BLOCK)
            wc[half * BLOCK : (half + 1) * BLOCK, rows] = wq_ref[half, rows, :].T
    dkv_acc[...] = jnp.zeros_like(dkv_acc)

    @pl.when(top_section)
    def _():
        load_top.wait()
        for k in range(CHUNKS):
            first = first_token(k)
            for i in range(4):
                g_buf[k, i] = top_ref[c_pos, first : first + ROWS, i * SLICE : (i + 1) * SLICE]

    for copy in kvt_copies:
        copy.wait_recv()
    keyval = kvt[...].T

    def pick(first_micro, second_micro):
        return jnp.where(c_pos == 0, first_micro.astype(F32), second_micro.astype(F32)).astype(BF16)

    mine = pick(kvt[:, :TOKENS], kvt[:, TOKENS:])
    k_t[...] = mine[:HEAD_DIM]
    v_t[...] = mine[HEAD_DIM:]
    mine = pick(keyval[:TOKENS], keyval[TOKENS:])
    k_low[...] = mine[:, :HEAD_DIM]
    v_low[...] = mine[:, HEAD_DIM:]
    for k in range(CHUNKS):
        first = first_token(k)
        scores = dot(q_low[k], k_t[...]) * SCALE
        row = lax.rem(lax.broadcasted_iota(jnp.int32, scores.shape, 0), ROWS) + first
        scores = jnp.where(row >= lax.broadcasted_iota(jnp.int32, scores.shape, 1), scores, -1e30)
        scores = jnp.exp(scores - jnp.max(scores, axis=-1, keepdims=True))
        probs = scores / jnp.sum(scores, axis=-1, keepdims=True)
        p_buf[k] = probs
        p_low_t[k] = probs.T.astype(BF16)
        attended = rows_to_heads(dot(probs.astype(BF16), v_low[...]))
        left, right = attended[:, :BLOCK], attended[:, BLOCK:]
        att_own[k] = jnp.where(c_pos == 0, left, right).astype(BF16)
        att_send[k] = jnp.where(c_pos == 0, right, left).astype(BF16)
    share_att = remote(att_send, att_in, att_sem.at[0], att_sem.at[1], s, peer(0, 0, 1))
    share_att.start()

    load_o.wait()
    share_o.wait_recv()
    for half in range(2):
        for b in range(WIDTH // BLOCK):
            rows = slice(b * BLOCK, (b + 1) * BLOCK)
            wot[rows, half * BLOCK : (half + 1) * BLOCK] = wo_ref[half, :, rows].T

    @pl.when(s < SECTIONS - 4)
    def _():
        pl.semaphore_wait(gate, 1)
        for i in range(PIECES):
            across(own_row, i).start()

    for i in range(PIECES):
        across(far_row, i).wait_recv()
        beside(far_row, i, PIECES + i).start()

    for i in range(PIECES):
        beside(near_row, i, i).wait_recv()
        beside(cross_row, i, PIECES + i).wait_recv()

    def ag_copy(k, dx):
        return remote(
            ag_buf.at[k], g_buf.at[k, x_pos], ag_send.at[k], ag_recv.at[k], s - 1, peer(dx, 0, 0)
        )

    def share_g(k):
        return remote(g_buf.at[k], g_in.at[k], g_send.at[k], g_recv.at[k], s, peer(0, 0, 1))

    def share_result(k):
        return remote(
            side_buf.at[k], side_in.at[k], side_send.at[k], side_recv.at[k], s, peer(0, 0, 1)
        )

    def first_half(k):
        first = pl.multiple_of(first_token(k), ROWS)

        @pl.when(s < SECTIONS - 1)
        def _():
            all_of(g_buf.at[k], ag_recv.at[k]).wait()

        g = jnp.concatenate([g_buf[k, i] for i in range(4)], axis=1)
        og = heads_to_rows(dot(g, wot[...]).astype(BF16))
        prob_grad = dot(og, v_t[...])
        probs = p_buf[k]
        delta = jnp.sum(probs * prob_grad, axis=-1, keepdims=True)
        score_grad = (probs * (prob_grad - delta)).astype(BF16)
        dq = (dot(score_grad, k_low[...]) * SCALE).astype(BF16)
        dkv_acc[:, :HEAD_DIM] += dot(score_grad, q_low[k], 0, 0) * SCALE
        dkv_acc[:, HEAD_DIM:] += dot(p_low_t[k], og)
        dkv = dkv_acc[pl.ds(first, ROWS), :].astype(BF16)
        keyval = jnp.concatenate(
            [k_low[pl.ds(first, ROWS), :], v_low[pl.ds(first, ROWS), :]], axis=1
        )
        stat = jnp.sum(rows_to_heads(dq.astype(F32) * q_hat[k]), axis=-1, keepdims=True)
        stat += jnp.sum(dkv.astype(F32) * keyval.astype(F32), axis=-1, keepdims=True)
        r = r_buf[c_pos, pl.ds(first, ROWS), :]
        stat = stat * (r * r / WIDTH)
        grads = jnp.concatenate([rows_to_heads(dq), dkv], axis=1)
        for j, dx in enumerate(HOPS):
            block = pl.ds(pl.multiple_of((x_pos + dx) % 4 * SLICE, SLICE), SLICE)
            part = dot(grads, wc[:, block]) * (r * gain_ref[:, block].astype(F32))
            part -= x_ref[c_pos, pl.ds(first, ROWS), block].astype(F32) * stat
            part_buf[k, j] = part.astype(BF16)
            for dz in (1, 0):
                if (dx, dz) == (0, 0):
                    continue
                remote(
                    part_buf.at[k, j], rs_buf.at[k, PEERS.index((dx, dz))],
                    rs_send.at[k], rs_recv.at[k], s, peer(dx, dz, 0),
                ).start()
        share_g(k).start()

    def second_half(k):
        first = pl.multiple_of(first_token(k), ROWS)
        total = g_buf[k, x_pos].astype(F32) + part_buf[k, len(HOPS) - 1].astype(F32)
        all_of(rs_buf.at[k], rs_recv.at[k]).wait()
        for j in range(len(PEERS)):
            total += rs_buf[k, j].astype(F32)
        ag_buf[k] = total.astype(BF16)

        @pl.when(s > 0)
        def _():
            for dx in HOPS:
                ag_copy(k, dx).start()

        half = jnp.where(z_pos == 0, total[:, : 2 * BLOCK], total[:, 2 * BLOCK :])
        left, right = half[:, :BLOCK], half[:, BLOCK:]
        side_buf[k] = jnp.where(c_pos == 0, right, left).astype(BF16)
        share_result(k).start()
        out_ref[c_pos, pl.ds(first, ROWS), :] = jnp.where(c_pos == 0, left, right).astype(BF16)

    def step(k, carry):
        @pl.when(k < CHUNKS)
        def _():
            first_half(k)

        @pl.when(k >= LAG)
        def _():
            second_half(k - LAG)

        return carry

    lax.fori_loop(0, CHUNKS + LAG, step, 0)

    @pl.when(s >= 4)
    def _():
        pl.semaphore_signal(gate, inc=1, device_id=(s - 4, d), device_id_type=MESH)

    share_att.wait_recv()
    att_out[c_pos] = att_own[...]
    att_out[other] = att_in[...]
    g_out[c_pos] = g_buf[...]
    for k in range(CHUNKS):
        share_g(k).wait_recv()
        g_out[other, k] = g_in[k]
    for k in range(CHUNKS):
        first = first_token(k)
        share_result(k).wait_recv()
        out_ref[other, first : first + ROWS, :] = side_in[k]

    for copy in (*kvt_copies, share_q, share_o, share_att):
        copy.wait_send()
    for i in range(PIECES):
        across(own_row, i).wait_send()
        beside(own_row, i, i).wait_send()
        beside(far_row, i, PIECES + i).wait_send()

    def drain(k, carry):
        all_of(rs_buf.at[k], rs_send.at[k]).wait()
        share_g(k).wait_send()
        share_result(k).wait_send()

        @pl.when(s > 0)
        def _():
            all_of(g_buf.at[k], ag_send.at[k]).wait()

        return carry

    lax.fori_loop(0, CHUNKS, drain, 0)


def relay(x, top, wq, wkv, wo, gain):
    vmem = pl.BlockSpec(memory_space=pltpu.VMEM)
    hbm = pl.BlockSpec(memory_space=pl.ANY)
    dma = pltpu.SemaphoreType.DMA
    return pl.pallas_call(
        kernel,
        out_shape=(
            jax.ShapeDtypeStruct((MICRO, TOKENS, BLOCK), BF16),
            jax.ShapeDtypeStruct((MICRO, CHUNKS, ROWS, BLOCK), BF16),
            jax.ShapeDtypeStruct((MICRO, CHUNKS, 4, ROWS, SLICE), BF16),
        ),
        in_specs=[hbm] * 5 + [vmem],
        out_specs=(vmem, vmem, vmem),
        scratch_shapes=[
            pltpu.VMEM((MICRO, TOKENS, WIDTH), BF16),
            pltpu.VMEM((MICRO, TOKENS, WIDTH), BF16),
            pltpu.VMEM((2, WIDTH, BLOCK), BF16),
            pltpu.VMEM((2, BLOCK, WIDTH), BF16),
            pltpu.VMEM((KV_ROW + BLOCK, WIDTH), BF16),
            pltpu.VMEM((WIDTH, KV_ROW), BF16),
            pltpu.VMEM((MICRO, TOKENS, WIDTH), BF16),
            pltpu.VMEM((MICRO, TOKENS, 1), F32),
            pltpu.VMEM((CHUNKS, HEADS * ROWS, HEAD_DIM), F32),
            pltpu.VMEM((CHUNKS, HEADS * ROWS, HEAD_DIM), BF16),
            pltpu.VMEM((BLOCK, MICRO * TOKENS), BF16),
            pltpu.VMEM((HEAD_DIM, TOKENS), BF16),
            pltpu.VMEM((HEAD_DIM, TOKENS), BF16),
            pltpu.VMEM((TOKENS, HEAD_DIM), BF16),
            pltpu.VMEM((TOKENS, HEAD_DIM), BF16),
            pltpu.VMEM((CHUNKS, HEADS * ROWS, TOKENS), F32),
            pltpu.VMEM((CHUNKS, TOKENS, HEADS * ROWS), BF16),
            pltpu.VMEM((TOKENS, BLOCK), F32),
            pltpu.VMEM((CHUNKS, 4, ROWS, SLICE), BF16),
            pltpu.VMEM((CHUNKS, 4, ROWS, SLICE), BF16),
            pltpu.VMEM((CHUNKS, ROWS, BLOCK), BF16),
            pltpu.VMEM((CHUNKS, ROWS, BLOCK), BF16),
            pltpu.VMEM((CHUNKS, ROWS, BLOCK), BF16),
            pltpu.VMEM((CHUNKS, len(HOPS), ROWS, SLICE), BF16),
            pltpu.VMEM((CHUNKS, len(PEERS), ROWS, SLICE), BF16),
            pltpu.VMEM((CHUNKS, ROWS, SLICE), BF16),
            pltpu.VMEM((CHUNKS, ROWS, BLOCK), BF16),
            pltpu.VMEM((CHUNKS, ROWS, BLOCK), BF16),
            dma((5,)),
            dma((CHUNKS,)),
            dma((CHUNKS,)),
            dma((CHUNKS,)),
            dma((CHUNKS,)),
            dma((2,)),
            dma((2,)),
            dma((CHUNKS,)),
            dma((CHUNKS,)),
            dma((CHUNKS,)),
            dma((CHUNKS,)),
            dma((2,)),
            dma((3,)),
            dma((3,)),
            dma((PIECES,)),
            dma((PIECES,)),
            dma((2 * PIECES,)),
            dma((2 * PIECES,)),
            pltpu.SemaphoreType.REGULAR,
        ],
        compiler_params=pltpu.CompilerParams(
            collective_id=0, has_side_effects=True, vmem_limit_bytes=60 * 1024 * 1024
        ),
        name="relay",
    )(x, top, wq, wkv, wo, gain)


def weight_kernel(block_ref, att_ref, g_ref, grad_ref):
    attended = att_ref[...].reshape(MICRO * TOKENS, BLOCK)
    g = g_ref[...].reshape(MICRO * TOKENS, SLICE)
    grad_ref[...] = dot(attended, g, 0, 0) * block_ref[0].astype(F32)


def weight_grad(new_block, att, g):
    return pl.pallas_call(
        weight_kernel,
        out_shape=jax.ShapeDtypeStruct((BLOCK, WIDTH), F32),
        grid=(4,),
        in_specs=[
            pl.BlockSpec(memory_space=pltpu.SMEM),
            pl.BlockSpec((MICRO, CHUNKS, ROWS, BLOCK), lambda i: (0, 0, 0, 0)),
            pl.BlockSpec((MICRO, CHUNKS, 1, ROWS, SLICE), lambda i: (0, 0, i, 0, 0)),
        ],
        out_specs=pl.BlockSpec((BLOCK, SLICE), lambda i: (0, i)),
        compiler_params=pltpu.CompilerParams(vmem_limit_bytes=16 * 1024 * 1024),
        name="weight_grad",
    )(new_block, att, g)


def body(layer_inputs, top_grad, w_query, w_keyval, w_out, norm_gain, new_block):
    stream, att, g = relay(
        layer_inputs[0], top_grad, w_query[0], w_keyval[0].T, w_out[0], norm_gain
    )
    return stream[None], weight_grad(new_block, att, g)[None]


def solution(mesh):
    in_specs = (
        P("section", None, None, None),
        P(),
        P("section", None, "dp"),
        P("section", None, "dp"),
        P("section", "dp", None),
        P("section", None),
        P("section"),
    )
    out_specs = (P("section", None, None, "dp"), P("section", "dp", None))
    return jax.shard_map(body, mesh=mesh, in_specs=in_specs, out_specs=out_specs, check_vma=False)
```

time: 293 us -> 271 us (0.925)
  Pallas kernels: 288 us -> 267 us
    pallas_call x1, Pallas kernels: 285 us -> 264 us  [relay(): pl.pallas_call(kernel, out_shape=(jax.ShapeDtypeStruct((MICRO, TOKENS, BL...]
where the time goes in v3:
time: 271 us
  Pallas kernels  267 us (99%)
    pallas_call x1, Pallas kernels, relay(): pl.pallas_call(kernel, out_shape=(jax.ShapeDtypeStruct((MICRO, TOKENS, BL...  264 us

profile of v3, /device:TPU:1, one launch (start us, length us, event | category | flops | bytes accessed | tf_op | source)
XLA Modules:
  0.0 270.7 jit_solution(1670547428044428936)
XLA Ops:
  1.3 263.7 %relay.1 = (bf16[2,64,256]{2,1,0:T(8,128)(2,1)}, bf16[2,4,16,256]{3,2,1,0:T(8,128)(2,1)}, bf16[2,4,4,16,1024]{4,3,2,1,0:T(8,128)(2,1)}) custom-call(bf16[2,64,4096]{2,1,0:T(8,128)(2,1)} %bitcast.11, bf16[2,64,4096]{2,1,0:T(8,128)(2,1)} %top_hbm.1, bf16[4096,256]{1,0:T(8,128)(2,1)} %bitcast.9, bf16[64,4096]{1,0:T(8,128)(2,1)} %bitcast.12, ...), custom_call_target="tpu_custom_call" | custom-call | tf_op jit(solution)/shard_map/relay/pallas_call | solution.py:374
  265.0 0.0 copy-start
  265.0 1.2 copy-done
  266.2 0.0 copy-start.1
  266.2 0.8 copy-done.1
  267.0 0.0 copy-start.2
  267.0 3.0 %weight_grad.1 = f32[256,4096]{1,0:T(8,128)} custom-call(s32[1]{0:T(128)S(6)} %copy.10.block_ref, bf16[2,4,16,256]{3,2,1,0:T(8,128)(2,1)S(1)} %copy-done.1, bf16[2,4,4,16,1024]{4,3,2,1,0:T(8,128)(2,1)S(1)} %copy-done), custom_call_target="tpu_custom_call" | custom-call | tf_op jit(solution)/shard_map/weight_grad/pallas_call | solution.py:446
  270.0 0.0 copy-done.2
  270.0 0.6 copy.11
Async XLA Ops:
  265.0 1.2 copy-start
  266.2 0.8 copy-start.1
  267.0 3.0 %copy-start.2 = (bf16[2,64,256]{2,1,0:T(8,128)(2,1)S(1)}, bf16[2,64,256]{2,1,0:T(8,128)(2,1)}, u32[]{:S(2)}) copy-start(bf16[2,64,256]{2,1,0:T(8,128)(2,1)} %get-tuple-element.5) | copy-start | bytes 196612

commit v4 on v3

--- a/solution.py
+++ b/solution.py
@@ -296,7 +296,6 @@
                     part_buf.at[k, j], rs_buf.at[k, PEERS.index((dx, dz))],
                     rs_send.at[k], rs_recv.at[k], s, peer(dx, dz, 0),
                 ).start()
-        share_g(k).start()
 
     def second_half(k):
         first = pl.multiple_of(first_token(k), ROWS)
@@ -330,10 +329,8 @@
 
     lax.fori_loop(0, CHUNKS + LAG, step, 0)
 
-    @pl.when(s >= 4)
-    def _():
-        pl.semaphore_signal(gate, inc=1, device_id=(s - 4, d), device_id_type=MESH)
-
+    for k in range(CHUNKS):
+        share_g(k).start()
     share_att.wait_recv()
     att_out[c_pos] = att_own[...]
     att_out[other] = att_in[...]
@@ -365,6 +362,10 @@
         return carry
 
     lax.fori_loop(0, CHUNKS, drain, 0)
+
+    @pl.when(s >= 4)
+    def _():
+        pl.semaphore_signal(gate, inc=1, device_id=(s - 4, d), device_id_type=MESH)
 
 
 def relay(x, top, wq, wkv, wo, gain):
@@ -453,7 +454,7 @@
             pl.BlockSpec((MICRO, CHUNKS, 1, ROWS, SLICE), lambda i: (0, 0, i, 0, 0)),
         ],
         out_specs=pl.BlockSpec((BLOCK, SLICE), lambda i: (0, i)),
-        compiler_params=pltpu.CompilerParams(vmem_limit_bytes=16 * 1024 * 1024),
+        compiler_params=pltpu.CompilerParams(vmem_limit_bytes=60 * 1024 * 1024),
         name="weight_grad",
     )(new_block, att, g)
 

time: 271 us -> 264 us (0.974)
  Pallas kernels: 267 us -> 261 us
    pallas_call x1, Pallas kernels: 264 us -> 257 us  [relay(): pl.pallas_call(kernel, out_shape=(jax.ShapeDtypeStruct((MICRO, TOKENS, BL...]
where the time goes in v4:
time: 264 us; the launch traced here: 263 us
  Pallas kernels  261 us (99%)
    pallas_call x1, Pallas kernels, relay(): pl.pallas_call(kernel, out_shape=(jax.ShapeDtypeStruct((MICRO, TOKENS, BL...  257 us

profile of v4, /device:TPU:1, one launch (start us, length us, event | category | flops | bytes accessed | tf_op | source)
XLA Modules:
  0.0 263.3 jit_solution(5563657326584304836)
XLA Ops:
  1.3 256.9 %relay.1 = (bf16[2,64,256]{2,1,0:T(8,128)(2,1)}, bf16[2,4,16,256]{3,2,1,0:T(8,128)(2,1)}, bf16[2,4,4,16,1024]{4,3,2,1,0:T(8,128)(2,1)}) custom-call(bf16[2,64,4096]{2,1,0:T(8,128)(2,1)} %bitcast.11, bf16[2,64,4096]{2,1,0:T(8,128)(2,1)} %top_hbm.1, bf16[4096,256]{1,0:T(8,128)(2,1)} %bitcast.9, bf16[64,4096]{1,0:T(8,128)(2,1)} %bitcast.12, ...), custom_call_target="tpu_custom_call" | custom-call | tf_op jit(solution)/shard_map/relay/pallas_call | solution.py:375
  258.2 0.0 copy-start
  258.2 4.5 %weight_grad.1 = f32[256,4096]{1,0:T(8,128)} custom-call(s32[1]{0:T(128)S(6)} %copy.10.block_ref, bf16[2,4,16,256]{3,2,1,0:T(8,128)(2,1)} %get-tuple-element.6.att_ref, bf16[2,4,4,16,1024]{4,3,2,1,0:T(8,128)(2,1)} %get-tuple-element.7.g_ref), custom_call_target="tpu_custom_call" | custom-call | tf_op jit(solution)/shard_map/weight_grad/pallas_call | solution.py:447
  262.7 0.0 copy-done
  262.7 0.6 copy.11
Async XLA Ops:
  258.2 4.5 %copy-start = (bf16[2,64,256]{2,1,0:T(8,128)(2,1)S(1)}, bf16[2,64,256]{2,1,0:T(8,128)(2,1)}, u32[]{:S(2)}) copy-start(bf16[2,64,256]{2,1,0:T(8,128)(2,1)} %get-tuple-element.5) | copy-start | bytes 196612
